TPU v7x, 32 devices: a whole 2x2x4 slice. The times are simulated.
32 devices in a mesh: lon: 8 (over z, core), lat: 4 (over y, x).
Axes of the slice: x: 2, y: 2, z: 4, core: 2. Of those that a mesh axis runs over, the one named last changes fastest.
Arguments:
- tracers: float32 [4, 512, 256, 128], P(None, 'lon', 'lat'), may hold values from 0.2 to 2
- kdiff: float32 [512, 256, 128], P('lon', 'lat'), may hold values from 0.3 to 8
- photolysis: float32 [512, 256, 128], P('lon', 'lat'), may hold values from 0.05 to 2
- u_wind: float32 [512, 256, 128], P('lon', 'lat'), may hold values from -0.24 to 0.24
- v_wind: float32 [512, 256, 128], P('lon', 'lat'), may hold values from -0.24 to 0.24
- day_count: int32 [8, 4], replicated, may hold values from 0 to 32, as said below
- day_order: int32 [8, 4, 32], P('lon', 'lat'), may hold values from 0 to 31, each once within a row
Outputs:
- tracers_next: float32 [4, 512, 256, 128], P(None, 'lon', 'lat')
Inputs may be any that keep to these rules, and one draw needn't show every extreme that they name: Tile (i, j) has day_count[i, j] daylit blocks, named by the first entries of day_order[i, j, :].
All inputs are finite; a program needn't handle non-finite values.
Results may differ from a plain program's by a relative error of at most 0.00002.
Values sent between devices are 32-bit elements; how exact they have to be, the bound alone decides.
No kernel may reach another device: no remote copies, remote signals or barrier semaphores. Data moves between devices by JAX's collectives and lax.ppermute only.
A program may use at most 128 MiB of HBM per device.

v0:
```python
import math

import jax
import jax.numpy as jnp
from jax import lax
from jax.sharding import PartitionSpec as P

SECTIONS = 12


def with_halo(cells, sides, width, closed):
    for axis, dim in sides:
        count = lax.axis_size(axis)
        ends = count if closed else count - 1
        head = lax.slice_in_dim(cells, 0, width, axis=dim)
        tail = lax.slice_in_dim(cells, cells.shape[dim] - width, cells.shape[dim], axis=dim)
        cells = jnp.concatenate(
            [
                lax.ppermute(tail, axis, [(i, (i + 1) % count) for i in range(ends)]),
                cells,
                lax.ppermute(head, axis, [((i + 1) % count, i) for i in range(ends)]),
            ],
            axis=dim,
        )
    return cells


def section_table(sections):
    bvals = [1.0 / 3.0] * 3 + [
        (j * j + j - 2.0) / (2.0 * j * (j + 1.0)) for j in range(3, sections + 1)
    ]
    scale = 4.0 / (sections * sections + sections - 2.0)
    rows = []
    for j in range(2, sections + 1):
        coef_prev = (2.0 * j - 1.0) / j * bvals[j] / bvals[j - 1]
        coef_back = -(j - 1.0) / j * bvals[j] / bvals[j - 2]
        coef_step = coef_prev * scale
        coef_first = -(1.0 - bvals[j - 1]) * coef_step
        rows.append((coef_prev, coef_back, 1.0 - coef_prev - coef_back, coef_step, coef_first))
    return (bvals[1] * scale, rows)


def tendency(field, diffusion, photo):
    above = jnp.concatenate([field[..., 1:], field[..., -1:]], axis=-1)
    upward = diffusion * (above - field)
    below = jnp.concatenate([jnp.zeros_like(upward[..., :1]), upward[..., :-1]], axis=-1)
    mixing = upward - below
    ozone, oxygen, nitric, dioxide = (field[0], field[1], field[2], field[3])
    titration = ozone * nitric
    split_no2 = 2.0 * photo * dioxide
    split_o3 = 0.25 * photo * ozone
    chemistry = jnp.stack(
        [
            1.5 * oxygen - titration - split_o3,
            split_no2 + split_o3 - 1.5 * oxygen,
            split_no2 - titration,
            titration - split_no2,
        ],
        axis=0,
    )
    return mixing + 0.5 * chemistry


def column_step(field, diffusion, photo):
    first_coef, table = section_table(SECTIONS)
    start_rate = tendency(field, diffusion, photo)
    previous = field
    current = field + first_coef * start_rate
    for coef_prev, coef_back, coef_base, coef_step, coef_first in table:
        following = (
            coef_prev * current
            + coef_back * previous
            + coef_base * field
            + coef_step * tendency(current, diffusion, photo)
            + coef_first * start_rate
        )
        previous, current = (current, following)
    return current


def night_step(field):
    ozone, oxygen, nitric = (field[0], field[1], field[2])
    titration = ozone * nitric
    change = jnp.stack([1.5 * oxygen - titration, -1.5 * oxygen, -titration, titration], axis=0)
    return field + 0.5 * change


def pick_blocks(blocks, diff_blocks, photo_blocks, block_ids):
    return jnp.concatenate(
        [
            jnp.take(blocks, block_ids, axis=1),
            jnp.take(diff_blocks, block_ids, axis=0)[None],
            jnp.take(photo_blocks, block_ids, axis=0)[None],
        ],
        axis=0,
    )


def advance_parcel(parcel, species):
    return column_step(parcel[:species], parcel[species], parcel[species + 1])


def local_pass(totals, blocks, diff_blocks, photo_blocks, ordering, slot_count, group_slots):
    species = blocks.shape[0]
    block_count = ordering.shape[0]
    turns = (slot_count + group_slots - 1) // group_slots

    def one_turn(turn, running):
        slots = turn * group_slots + jnp.arange(group_slots, dtype=jnp.int32)
        valid = slots < slot_count
        block_ids = ordering[jnp.clip(slots, 0, block_count - 1)]
        parcel = pick_blocks(blocks, diff_blocks, photo_blocks, block_ids)
        advanced = advance_parcel(parcel, species)
        targets = jnp.where(valid, block_ids, block_count)
        return running.at[:, targets].set(advanced, mode="drop")

    return lax.fori_loop(jnp.int32(0), turns, one_turn, totals)


def body(tracers, kdiff, photolysis, u_wind, v_wind, day_count, day_order):
    species, lon_cells, lat_cells, levels = tracers.shape
    ordering = day_order[0, 0]
    block_count = ordering.shape[0]
    block_cols = lon_cells * lat_cells // block_count
    half_slots = block_count // 2
    group_slots = math.gcd(4, half_slots)
    lon_place = lax.axis_index("lon")
    lat_place = lax.axis_index("lat")
    own_count = day_count[lon_place, lat_place]
    blocks = tracers.reshape(species, block_count, block_cols, levels)
    diff_blocks = kdiff.reshape(block_count, block_cols, levels)
    photo_blocks = photolysis.reshape(block_count, block_cols, levels)
    stepped = night_step(blocks)
    stepped = local_pass(
        stepped, blocks, diff_blocks, photo_blocks, ordering, own_count, group_slots
    )
    current = stepped.reshape(species, lon_cells, lat_cells, levels)
    lon_ext = with_halo(jnp.concatenate([current, u_wind[None]], axis=0), (("lon", 1),), 1, True)
    lat_ext = with_halo(jnp.concatenate([current, v_wind[None]], axis=0), (("lat", 2),), 1, False)
    tracer_lon, u_ext = (lon_ext[:species], lon_ext[species])
    tracer_lat, v_ext = (lat_ext[:species], lat_ext[species])
    face_x = (
        jnp.maximum(u_ext[:-1], 0.0) * tracer_lon[:, :-1]
        + jnp.minimum(u_ext[:-1], 0.0) * tracer_lon[:, 1:]
    )
    east = face_x[:, 1:]
    west = face_x[:, :-1]
    face_y = (
        jnp.maximum(v_ext[:, :-1], 0.0) * tracer_lat[:, :, :-1]
        + jnp.minimum(v_ext[:, :-1], 0.0) * tracer_lat[:, :, 1:]
    )
    north = face_y[:, :, 1:]
    south = face_y[:, :, :-1]
    return current - (east - west) - (north - south)


def solution(mesh):
    return jax.shard_map(
        body,
        mesh=mesh,
        in_specs=(
            P(None, "lon", "lat", None),
            P("lon", "lat", None),
            P("lon", "lat", None),
            P("lon", "lat", None),
            P("lon", "lat", None),
            P(),
            P("lon", "lat", None),
        ),
        out_specs=P(None, "lon", "lat", None),
        check_vma=False,
    )
```

profile of v0, /device:TPU:0, one launch (start us, length us, event | category | flops | bytes accessed | tf_op | source)
XLA Modules:
  0.0 377.4 jit_solution(12424706542429246165)
XLA Ops:
  1.8 6.3 %slice_multiply_fusion.14 = (f32[1,64,64,128]{3,2,1,0:T(8,128)}, f32[1,64,64,128]{3,2,1,0:T(8,128)}, f32[1,64,64,128]{3,2,1,0:T(8,128)S(1)}) fusion(f32[4,64,64,128]{3,2,1,0:T(8,128)} %param.11), kind=kLoop, calls=%fused_computation.288 | loop fusion | flops 1572864 | bytes 12582912 | tf_op jit(solution)/shard_map/mul | solution.py:84
  8.1 2.3 bitcast_subtract_fusion
  10.4 6.6 %fusion.114 = f32[4,32,128,128]{3,2,1,0:T(8,128)} fusion(f32[1,32,128,128]{3,2,1,0:T(8,128)S(1)} %bitcast.863, f32[1,32,128,128]{3,2,1,0:T(8,128)S(1)} %get-tuple-element.133, f32[1,32,128,128]{3,2,1,0:T(8,128)S(1)} %bitcast.864, f32[1,32,128,128]{3,2,1,0:T(8,128)S(1)} %get-tuple-element.132, f32[4,32,128,128]{3,2,1,0:T(8,128)} %bitcast.854), kind=kLoop, calls=%fused_computation.275 | loop fusion | flops 10485760 | bytes 25165824 | tf_op jit(solution)/shard_map/add | solution.py:85
  17.0 316.1 %while.10 = (s32[]{:T(128)}, f32[4,32,128,128]{3,2,1,0:T(8,128)}, s32[]{:T(128)}, s32[]{:T(128)}, s32[32]{0:T(128)S(1)}, /*index=5*/f32[4,32,128,128]{3,2,1,0:T(...) while((s32[]{:T(128)}, f32[4,32,128,128]{3,2,1,0:T(8,128)}, s32[]{:T(128)}, ...), condition=%wide.region_2.4_spmd, body=%wide.region_0.3_spmd.sunk | while | flops 70847584 | bytes 208057808 | solution.py:117
  18.3 2.2 gather_fusion.2
  20.4 2.2 gather_fusion.3
  22.6 4.0 %gather_fusion.1 = f32[4,4,128,128]{3,2,1,0:T(8,128)S(1)} fusion(f32[4,32,128,128]{3,2,1,0:T(8,128)} %get-tuple-element.319, s32[1024]{0:T(1024)S(1)} %pad_clamp_fusion.7), kind=kCustom, calls=%fused_computation.3.clone.1 | custom fusion | bytes 2097168 | tf_op jit(solution)/shard_map/while/body/jit(_take)/gather | solution.py:91
  51.7 1.7 fusion.175
  53.4 3.1 scatter_fusion
  57.8 2.2 gather_fusion.2
  60.0 2.2 gather_fusion.3
  62.1 4.0 %gather_fusion.1 = f32[4,4,128,128]{3,2,1,0:T(8,128)S(1)} fusion(f32[4,32,128,128]{3,2,1,0:T(8,128)} %get-tuple-element.319, s32[1024]{0:T(1024)S(1)} %pad_clamp_fusion.7), kind=kCustom, calls=%fused_computation.3.clone.1 | custom fusion | bytes 2097168 | tf_op jit(solution)/shard_map/while/body/jit(_take)/gather | solution.py:91
  91.2 1.7 fusion.175
  92.9 3.1 scatter_fusion
  97.3 2.2 gather_fusion.2
  99.5 2.2 gather_fusion.3
  101.6 4.0 %gather_fusion.1 = f32[4,4,128,128]{3,2,1,0:T(8,128)S(1)} fusion(f32[4,32,128,128]{3,2,1,0:T(8,128)} %get-tuple-element.319, s32[1024]{0:T(1024)S(1)} %pad_clamp_fusion.7), kind=kCustom, calls=%fused_computation.3.clone.1 | custom fusion | bytes 2097168 | tf_op jit(solution)/shard_map/while/body/jit(_take)/gather | solution.py:91
  130.7 1.7 fusion.175
  132.4 3.1 scatter_fusion
  136.8 2.2 gather_fusion.2
  139.0 2.2 gather_fusion.3
  141.2 4.0 %gather_fusion.1 = f32[4,4,128,128]{3,2,1,0:T(8,128)S(1)} fusion(f32[4,32,128,128]{3,2,1,0:T(8,128)} %get-tuple-element.319, s32[1024]{0:T(1024)S(1)} %pad_clamp_fusion.7), kind=kCustom, calls=%fused_computation.3.clone.1 | custom fusion | bytes 2097168 | tf_op jit(solution)/shard_map/while/body/jit(_take)/gather | solution.py:91
  170.2 1.7 fusion.175
  172.0 3.1 scatter_fusion
  176.4 2.2 gather_fusion.2
  178.5 2.2 gather_fusion.3
  180.7 4.0 %gather_fusion.1 = f32[4,4,128,128]{3,2,1,0:T(8,128)S(1)} fusion(f32[4,32,128,128]{3,2,1,0:T(8,128)} %get-tuple-element.319, s32[1024]{0:T(1024)S(1)} %pad_clamp_fusion.7), kind=kCustom, calls=%fused_computation.3.clone.1 | custom fusion | bytes 2097168 | tf_op jit(solution)/shard_map/while/body/jit(_take)/gather | solution.py:91
  209.8 1.7 fusion.175
  211.5 3.1 scatter_fusion
  215.9 2.2 gather_fusion.2
  218.0 2.2 gather_fusion.3
  220.2 4.0 %gather_fusion.1 = f32[4,4,128,128]{3,2,1,0:T(8,128)S(1)} fusion(f32[4,32,128,128]{3,2,1,0:T(8,128)} %get-tuple-element.319, s32[1024]{0:T(1024)S(1)} %pad_clamp_fusion.7), kind=kCustom, calls=%fused_computation.3.clone.1 | custom fusion | bytes 2097168 | tf_op jit(solution)/shard_map/while/body/jit(_take)/gather | solution.py:91
  249.3 1.7 fusion.175
  251.0 3.1 scatter_fusion
  255.4 2.2 gather_fusion.2
  257.6 2.2 gather_fusion.3
  259.7 4.0 %gather_fusion.1 = f32[4,4,128,128]{3,2,1,0:T(8,128)S(1)} fusion(f32[4,32,128,128]{3,2,1,0:T(8,128)} %get-tuple-element.319, s32[1024]{0:T(1024)S(1)} %pad_clamp_fusion.7), kind=kCustom, calls=%fused_computation.3.clone.1 | custom fusion | bytes 2097168 | tf_op jit(solution)/shard_map/while/body/jit(_take)/gather | solution.py:91
  290.5 3.1 scatter_fusion
  294.9 2.2 gather_fusion.2
  297.1 2.2 gather_fusion.3
  299.3 4.0 %gather_fusion.1 = f32[4,4,128,128]{3,2,1,0:T(8,128)S(1)} fusion(f32[4,32,128,128]{3,2,1,0:T(8,128)} %get-tuple-element.319, s32[1024]{0:T(1024)S(1)} %pad_clamp_fusion.7), kind=kCustom, calls=%fused_computation.3.clone.1 | custom fusion | bytes 2097168 | tf_op jit(solution)/shard_map/while/body/jit(_take)/gather | solution.py:91
  330.0 3.0 scatter_fusion
  333.1 2.1 fusion.116
  336.8 4.6 %collective-permute-start.2 = (f32[5,64,1,128]{3,1,2,0:T(8,128)S(1)}, f32[5,64,1,128]{3,1,2,0:T(8,128)S(1)}, u32[]{:S(2)}, u32[]{:S(2)}) collective-permute-start(f32[5,64,1,128]{3,1,2,0:T(8,128)S(1)} %bitcast.872), channel_id=1, source_target_pairs={{0,1},{1,2},{2,3},{4,5},{5,6},{6,7},{8,9},{9,10},{10,11},{12,13},{... | collective-permute-start | bytes 491528 | tf_op jit(solution)/shard_map/ppermute | solution.py:19
  341.5 4.0 %collective-permute-start.1 = (f32[5,1,64,128]{3,2,1,0:T(8,128)S(1)}, f32[5,1,64,128]{3,2,1,0:T(8,128)S(1)}, u32[]{:S(2)}, u32[]{:S(2)}) collective-permute-start(f32[5,1,64,128]{3,2,1,0:T(8,128)S(1)} %get-tuple-element.124), channel_id=1, source_target_pairs={{4,0},{8,4},{12,8},{16,12},{20,16},{24,20},{28,24},{0,28},{5,1},{9... | collective-permute-start | bytes 491528 | tf_op jit(solution)/shard_map/ppermute | solution.py:21
  346.1 5.9 %fusion.107 = f32[4,64,65,128]{3,2,1,0:T(8,128)} fusion(f32[5,64,1,128]{3,2,1,0:T(1,128)S(1)} %bitcast.869, f32[1,64,64,128]{3,2,1,0:T(8,128)S(1)} %bitcast.858, f32[4,64,64,128]{3,2,1,0:T(8,128)S(1)} %bitcast.839, f32[5,64,1,128]{3,2,1,0:T(1,128)S(1)} %bitcast.871, f32[64,65,128]{2,1,0:T(8,128)S(1)} %get-tuple-element.131, ...), kind=kLoop, calls=%fused_computation.258 | loop fusion | flops 14909440 | bytes 23592960 | tf_op jit(solution)/shard_map/add | solution.py:149
  352.6 5.2 %fusion.110 = f32[4,65,64,128]{3,2,1,0:T(8,128)} fusion(f32[5,1,64,128]{3,2,1,0:T(8,128)S(1)} %collective-permute-done.1, f32[1,64,64,128]{3,2,1,0:T(8,128)S(1)} %bitcast.861, f32[4,64,64,128]{3,2,1,0:T(8,128)S(1)} %bitcast.841, f32[5,1,64,128]{3,2,1,0:T(8,128)S(1)} %collective-permute-done, f32[65,64,128]{2,1,0:T(8,128)S(1)} %minimum_bitcast_fusion, ...), kind=kLoop, calls=%fused_computation.265 | loop fusion | flops 14909440 | bytes 23592960 | tf_op jit(solution)/shard_map/add | solution.py:143
  357.8 19.6 %fusion.112 = f32[4,64,64,128]{3,2,1,0:T(8,128)} fusion(f32[4,64,65,128]{3,2,1,0:T(8,128)} %fusion.107, f32[4,64,64,128]{3,2,1,0:T(8,128)} %bitcast.836, f32[4,65,64,128]{3,2,1,0:T(8,128)} %fusion.110), kind=kLoop, calls=%fused_computation.271 | loop fusion | flops 8388608 | bytes 50331648 | tf_op jit(solution)/shard_map/sub | solution.py:154
  (608 shorter events, 215.9 us)
Async XLA Ops:
  8.1 2.3 copy-start.4
  10.4 6.6 %copy-start = (s32[1,1,32]{2,1,0:T(1,128)S(1)}, s32[1,1,32]{2,1,0:T(1,128)}, u32[]{:S(2)}) copy-start(s32[1,1,32]{2,1,0:T(1,128)} %param.17) | copy-start | bytes 388
  333.1 8.3 %copy-start.1 = (f32[4,32,128,128]{3,2,1,0:T(8,128)S(1)}, f32[4,32,128,128]{3,2,1,0:T(8,128)}, u32[]{:S(2)}) copy-start(f32[4,32,128,128]{3,2,1,0:T(8,128)} %get-tuple-element.49) | copy-start | bytes 25165828
  333.1 8.3 %copy-start.3 = (f32[64,64,128]{2,1,0:T(8,128)S(1)}, f32[64,64,128]{2,1,0:T(8,128)}, u32[]{:S(2)}) copy-start(f32[64,64,128]{2,1,0:T(8,128)} %param.14) | copy-start | bytes 6291460
  333.1 12.4 %copy-start.2 = (f32[64,64,128]{2,1,0:T(8,128)S(1)}, f32[64,64,128]{2,1,0:T(8,128)}, u32[]{:S(2)}) copy-start(f32[64,64,128]{2,1,0:T(8,128)} %param.15) | copy-start | bytes 6291460
  335.2 10.2 %collective-permute-start.3 = (f32[5,64,1,128]{3,1,2,0:T(8,128)S(1)}, f32[5,64,1,128]{3,1,2,0:T(8,128)S(1)}, u32[]{:S(2)}, u32[]{:S(2)}) collective-permute-start(f32[5,64,1,128]{3,1,2,0:T(8,128)S(1)} %bitcast.873), channel_id=1, source_target_pairs={{1,0},{2,1},{3,2},{5,4},{6,5},{7,6},{9,8},{10,9},{11,10},{13,12},{... | collective-permute-start | bytes 491528 | tf_op jit(solution)/shard_map/ppermute | solution.py:21
  336.8 8.7 %collective-permute-start.2 = (f32[5,64,1,128]{3,1,2,0:T(8,128)S(1)}, f32[5,64,1,128]{3,1,2,0:T(8,128)S(1)}, u32[]{:S(2)}, u32[]{:S(2)}) collective-permute-start(f32[5,64,1,128]{3,1,2,0:T(8,128)S(1)} %bitcast.872), channel_id=1, source_target_pairs={{0,1},{1,2},{2,3},{4,5},{5,6},{6,7},{8,9},{9,10},{10,11},{12,13},{... | collective-permute-start | bytes 491528 | tf_op jit(solution)/shard_map/ppermute | solution.py:19
  341.4 10.6 %collective-permute-start = (f32[5,1,64,128]{3,2,1,0:T(8,128)S(1)}, f32[5,1,64,128]{3,2,1,0:T(8,128)S(1)}, u32[]{:S(2)}, u32[]{:S(2)}) collective-permute-start(f32[5,1,64,128]{3,2,1,0:T(8,128)S(1)} %get-tuple-element.123), channel_id=1, source_target_pairs={{0,4},{4,8},{8,12},{12,16},{16,20},{20,24},{24,28},{28,0},{1,5},{5... | collective-permute-start | bytes 491528 | tf_op jit(solution)/shard_map/ppermute | solution.py:19
  341.5 11.2 %collective-permute-start.1 = (f32[5,1,64,128]{3,2,1,0:T(8,128)S(1)}, f32[5,1,64,128]{3,2,1,0:T(8,128)S(1)}, u32[]{:S(2)}, u32[]{:S(2)}) collective-permute-start(f32[5,1,64,128]{3,2,1,0:T(8,128)S(1)} %get-tuple-element.124), channel_id=1, source_target_pairs={{4,0},{8,4},{12,8},{16,12},{20,16},{24,20},{28,24},{0,28},{5,1},{9... | collective-permute-start | bytes 491528 | tf_op jit(solution)/shard_map/ppermute | solution.py:21
where the time goes:
time: 379 us; the launch traced here: 377 us
  other arithmetic  199 us (53%)
  local copies, waits for them, and re-layouts  165 us (44%)
  starting transfers between devices  10.2 us (3%)
    add x96, other arithmetic, column_step(): coef_prev * current + coef_back * previous + coef_base * field  84.3 us
    slice x192, local copies, waits for them, and re-layouts, tendency(): above = jnp.concatenate([field[..., 1:], field[..., -1:]], axis=-1)  64.7 us
    mul x88, other arithmetic, tendency(): upward = diffusion * (above - field)  35 us
    gather x8, local copies, waits for them, and re-layouts, pick_blocks(): jnp.take(blocks, block_ids, axis=1)  32 us
    scatter x8, local copies, waits for them, and re-layouts, one_turn(): return running.at[:, targets].set(advanced, mode='drop')  24.9 us
    sub x1, other arithmetic, body(): return current - (east - west) - (north - south)  19.6 us
    another operation x96, other arithmetic, tendency(): jnp.stack([1.5 * oxygen - titration - split_o3, split_no2 + split_o3 - 1....  19.5 us
    gather x8, local copies, waits for them, and re-layouts, pick_blocks(): jnp.take(photo_blocks, block_ids, axis=0)[None]  17.2 us
  transfers between devices with their start and end apart: 4, of which 0 were waited for; matrix products, arithmetic and copies ran while one was open for 2% of the time, Pallas kernels for 0%

commit v1 on v0

v1 whole, which is shorter than its diff:
```python
import jax
import jax.numpy as jnp
from jax import lax
from jax.experimental import pallas as pl
from jax.experimental.pallas import tpu as pltpu
from jax.sharding import PartitionSpec as P

SECTIONS = 12
SUB = 8
FIELDS = 6


def section_table(sections):
    bvals = [1.0 / 3.0] * 3 + [
        (j * j + j - 2.0) / (2.0 * j * (j + 1.0)) for j in range(3, sections + 1)
    ]
    rate = 4.0 / (sections * sections + sections - 2.0)
    scale = [1.0, 1.0]
    for j in range(2, sections + 1):
        scale.append(-(j - 1.0) / j * scale[j - 2])
    lead = [0.0, 0.0] + [
        (2.0 * j - 1.0) / j * scale[j - 1] / scale[j] for j in range(2, sections + 1)
    ]
    return bvals, rate, scale, lead


BVALS, RATE, SCALE, LEAD = section_table(SECTIONS)
HALF = 0.5 * RATE
OXYGEN = 1.5 * HALF


def stage_consts(j):
    b, scale = BVALS[j - 1], SCALE[j - 1]
    rho = (1.0 - b) / (b * scale)
    return LEAD[j], rho, HALF * b * scale, rho * HALF


def rows(i):
    return pl.ds(SUB * i, SUB)


def runs(i, steps):
    return pl.ds(i, SUB, stride=steps + 1)


def sweep(coef, steps, load, titration, finish):
    first, end = load(0), load(steps - 1)
    k_end = coef[0, rows(steps - 1), :]
    f_end = [k_end * (pltpu.roll(n, SUB - 1, axis=0) - c) for n, c in zip(first, end)]
    before = [pltpu.roll(f, 1, axis=0) for f in f_end]
    current = first
    for i in range(steps):
        if i < steps - 1:
            above = load(i + 1)
            k = coef[0, rows(i), :]
            flux = [k * (n - c) for n, c in zip(above, current)]
        else:
            above, flux = None, f_end
        t = titration(i, current)
        gain = [a - b for a, b in zip(flux, before)]
        ozone = (coef[2, rows(i), :] * current[0] + gain[0]) + (
            OXYGEN * (current[3] - current[1]) - t
        )
        dioxide = (coef[1, rows(i), :] * current[1] + gain[1]) + t
        finish(i, [ozone, dioxide, current[2] + gain[2], current[3] + gain[3]])
        current, before = above, flux


def prepare(i, steps, tin, state, coef):
    ozone, oxygen, nitric, dioxide, k, photo = (tin[s, runs(i, steps), :] for s in range(FIELDS))
    k = k * RATE
    if i == steps - 1:
        k = jnp.where(lax.broadcasted_iota(jnp.int32, k.shape, 0) == SUB - 1, 0.0, k)
    split = photo * (2.0 * HALF)
    odd = (ozone + oxygen) + dioxide
    for s, value in enumerate((ozone, dioxide, nitric + dioxide, odd, nitric)):
        state[s, rows(i), :] = value
    for s, value in enumerate((k, 1.0 - split, (1.0 - OXYGEN) - 0.125 * split, ozone * nitric)):
        coef[s, rows(i), :] = value


def conclude(i, steps, tout, state, bufs):
    base, weight = 1.0 - BVALS[SECTIONS], BVALS[SECTIONS] * SCALE[SECTIONS]
    ozone, dioxide, nitrogen, odd = (
        weight * bufs[SECTIONS % 2, s, rows(i), :] + base * state[s, rows(i), :] for s in range(4)
    )
    for s, value in enumerate((ozone, (odd - dioxide) - ozone, nitrogen - dioxide, dioxide)):
        tout[s, runs(i, steps), :] = value


def first_stage(steps, state, bufs, coef, exchange):
    ready = set()

    def load(i):
        if i not in ready:
            ready.add(i)
            exchange(i)
        return [state[s, rows(i), :] for s in range(4)]

    def finish(i, fields):
        for s in range(4):
            bufs[1, s, rows(i), :] = fields[s]

    sweep(coef, steps, load, lambda i, current: HALF * coef[3, rows(i), :], finish)


def later_stage(consts, steps, source, back, target, state, coef):
    lead, rho, kappa, base = consts

    def titration(i, current):
        left = kappa * (current[0] + rho * state[0, rows(i), :])
        right = (current[2] - current[1]) + rho * state[4, rows(i), :]
        return left * right - base * coef[3, rows(i), :]

    def finish(i, fields):
        for s in range(4):
            target[s, rows(i), :] = lead * fields[s] + back[s, rows(i), :]

    sweep(
        coef, steps, lambda i: [source[s, rows(i), :] for s in range(4)], titration, finish
    )


def column_kernel(
    counts, ranks, y, k, p, u, v, mix, lon_tail, lon_head, lat_tail, lat_head,
    raw, tin, tout, state, bufs, coef, wind, table, count, rank, flag, order, sem, wsem, ssem,
):
    species, blocks, cols, levels = y.shape
    lon_cells, lat_cells = u.shape[:2]
    steps = levels // SUB
    for j in range(3, SECTIONS + 1):
        for c, value in enumerate(stage_consts(j)):
            table[j - 3, c] = value

    def fetch(b, _):
        for src, dst in (
            (y.at[:, b], raw.at[pl.ds(0, species), b]),
            (k.at[b], raw.at[species, b]),
            (p.at[b], raw.at[species + 1, b]),
        ):
            pltpu.make_async_copy(src, dst, sem.at[b]).start()
        return 0

    def arrive(n):
        b = order[n]
        whole = raw.at[:, b]
        pltpu.make_async_copy(whole, whole, sem.at[b]).wait()
        return b

    def place(b):
        return pl.ds(pl.multiple_of(b * cols, cols), cols)

    def bring(s, b):
        x = raw[s, b].T
        for g in range(SUB):
            tin[s, pl.ds(g * (steps + 1), steps), :] = x[g * steps : (g + 1) * steps, :]

    def emit(s, b):
        x = jnp.concatenate(
            [tout[s, pl.ds(g * (steps + 1), steps), :] for g in range(SUB)], axis=0
        )
        mix[s, place(b), :] = x.T

    winds = (
        pltpu.make_async_copy(u.at[lon_cells - 1], lon_tail.at[species], wsem.at[0]),
        pltpu.make_async_copy(v.at[:, pl.ds(lat_cells - SUB, SUB)], wind, wsem.at[1]),
    )
    lists = (
        pltpu.make_async_copy(counts, count, ssem.at[0]),
        pltpu.make_async_copy(ranks, rank, ssem.at[1]),
    )
    for copy in lists:
        copy.start()
    lax.fori_loop(0, blocks, fetch, 0)
    for copy in winds:
        copy.start()
    for copy in lists:
        copy.wait()
    lit = count[lax.axis_index("lat"), lax.axis_index("lon")]

    def mark(n, _):
        flag[rank[0, 0, n]] = jnp.where(n < lit, 0, 1)
        return 0

    lax.fori_loop(0, blocks, mark, 0)

    def sort(b, ends):
        first, final = ends
        dark = flag[b]
        order[jnp.where(dark == 0, first, final)] = b
        return first + 1 - dark, final + dark

    lax.fori_loop(0, blocks, sort, (0, lit))

    @pl.when(lit > 0)
    def _():
        start = arrive(0)
        for s in range(FIELDS):
            bring(s, start)

        def turn(n, _):
            @pl.when(n + 1 < lit)
            def _():
                arrive(n + 1)

            coming = order[jnp.minimum(n + 1, lit - 1)]
            leaving = jnp.where(n > 0, order[jnp.maximum(n - 1, 0)], blocks)
            def exchange(i):
                conclude(i, steps, tout, state, bufs)
                prepare(i, steps, tin, state, coef)

            first_stage(steps, state, bufs, coef, exchange)
            bring(FIELDS - 1, coming)
            later_stage(stage_consts(2), steps, bufs.at[1], state, bufs.at[0], state, coef)

            def pair(turn_pair, _):
                bring(turn_pair, coming)
                emit(jnp.minimum(turn_pair, species - 1), leaving)
                for q in range(2):
                    consts = [table[2 * turn_pair + q, c] for c in range(4)]
                    now, other = bufs.at[q], bufs.at[1 - q]
                    later_stage(consts, steps, now, other, other, state, coef)
                return 0

            lax.fori_loop(0, (SECTIONS - 2) // 2, pair, 0)
            return 0

        lax.fori_loop(0, lit, turn, 0)
        for i in range(steps):
            conclude(i, steps, tout, state, bufs)
        for s in range(species):
            emit(s, order[lit - 1])

    def night(n, _):
        b = arrive(n)
        ozone, oxygen, nitric, dioxide = (raw[s, b] for s in range(species))
        t = 0.5 * (ozone * nitric)
        values = (ozone + (0.75 * oxygen - t), oxygen - 0.75 * oxygen, nitric - t, dioxide + t)
        for s, value in enumerate(values):
            mix[s, place(b), :] = value
        return 0

    lax.fori_loop(lit, blocks, night, 0)
    for copy in winds:
        copy.wait()
    for s in range(species):
        lon_head[s] = mix[s, pl.ds(0, lat_cells), :]
        lon_tail[s] = mix[s, pl.ds((lon_cells - 1) * lat_cells, lat_cells), :]
        for i in range(lon_cells // SUB):
            start = i * SUB * lat_cells
            lat_head[s, rows(i), :] = mix[s, pl.ds(start, SUB, stride=lat_cells), :]
            lat_tail[s, rows(i), :] = mix[s, pl.ds(start + lat_cells - 1, SUB, stride=lat_cells), :]
    flat = wind.reshape(lon_cells * SUB, levels)
    for i in range(lon_cells // SUB):
        lat_tail[species, rows(i), :] = flat[pl.ds(i * SUB * SUB + SUB - 1, SUB, stride=SUB), :]


def buffer(*dims):
    return pltpu.VMEM(dims, jnp.float32)


ANYWHERE = pl.BlockSpec(memory_space=pl.ANY)
VECTORS = pl.BlockSpec(memory_space=pltpu.VMEM)


def in_hbm(x):
    return pltpu.with_memory_space_constraint(x, pltpu.HBM)


def in_vmem(x):
    return pltpu.with_memory_space_constraint(x, pltpu.VMEM)


def column_pass(count, order, tracers, kdiff, photolysis, u_wind, v_wind):
    species, lon_cells, lat_cells, levels = tracers.shape
    blocks = order.shape[2]
    cols = lon_cells * lat_cells // blocks
    return pl.pallas_call(
        column_kernel,
        in_specs=[ANYWHERE] * 7,
        out_specs=[VECTORS] * 5,
        out_shape=[
            buffer(species, (blocks + 1) * cols, levels),
            buffer(species + 1, lat_cells, levels),
            buffer(species, lat_cells, levels),
            buffer(species + 1, lon_cells, levels),
            buffer(species, lon_cells, levels),
        ],
        scratch_shapes=[
            buffer(FIELDS, blocks, cols, levels),
            buffer(FIELDS, levels + SUB, cols),
            buffer(species, levels + SUB, cols),
            buffer(species + 1, levels, cols),
            buffer(2, species, levels, cols),
            buffer(4, levels, cols),
            buffer(lon_cells, SUB, levels),
            pltpu.SMEM((SECTIONS - 2, 4), jnp.float32),
            pltpu.SMEM(count.shape, jnp.int32),
            pltpu.SMEM(order.shape, jnp.int32),
            pltpu.SMEM((blocks,), jnp.int32),
            pltpu.SMEM((blocks,), jnp.int32),
            pltpu.SemaphoreType.DMA((blocks,)),
            pltpu.SemaphoreType.DMA((2,)),
            pltpu.SemaphoreType.DMA((2,)),
        ],
        compiler_params=pltpu.CompilerParams(vmem_limit_bytes=24 << 20),
        name="columns",
    )(
        in_hbm(count),
        in_hbm(order),
        in_hbm(tracers.reshape(species, blocks, cols, levels)),
        in_hbm(kdiff.reshape(blocks, cols, levels)),
        in_hbm(photolysis.reshape(blocks, cols, levels)),
        in_hbm(u_wind),
        in_hbm(v_wind),
    )


def transport_kernel(
    mix, u, v, out, lon_rim, lat_rim, east_flux, north_flux, stage, sem,
):
    lon_cells, lat_cells, levels = u.shape
    species = out.shape[0]
    tiles = lat_cells // SUB
    zero = jnp.zeros((SUB, levels), jnp.float32)
    row = lax.broadcasted_iota(jnp.int32, (SUB, levels), 0)
    for s in range(species):
        for q in range(2):
            north_flux[q, s, rows(0), :] = zero
        for t in range(tiles):
            east_flux[s, rows(t), :] = zero

    def line(i, q, last, put):
        base = pl.multiple_of(i * lat_cells, SUB)
        for t in range(tiles):
            wu, wv = u[i, rows(t), :], v[i, rows(t), :]
            east_going, north_going = wu > 0.0, wv > 0.0
            for s in range(species):
                here = mix[s, pl.ds(base + t * SUB, SUB), :]
                donor = 0.0 if last else mix[s, pl.ds(base + lat_cells + t * SUB, SUB), :]
                x_flux = wu * jnp.where(east_going, here, donor)
                if t < tiles - 1:
                    ahead = mix[s, pl.ds(base + t * SUB + 1, SUB), :]
                else:
                    ahead = jnp.where(row < SUB - 1, pltpu.roll(here, SUB - 1, axis=0), 0.0)
                y_flux = wv * jnp.where(north_going, here, ahead)
                north_flux[q, s, rows(t + 1), :] = y_flux
                x_loss = x_flux - east_flux[s, rows(t), :]
                east_flux[s, rows(t), :] = x_flux
                y_loss = y_flux - north_flux[q, s, pl.ds(t * SUB + SUB - 1, SUB), :]
                put(s, t, (here - x_loss) - y_loss)

    def rim_row(side):
        def put(s, t, value):
            lon_rim[s, side, rows(t), :] = value

        return put

    def inner_row(i):
        def put(s, t, value):
            if 0 < t < tiles - 1:
                stage[s, i - 1, rows(t - 1), :] = value
            else:
                lat_rim[s, min(t, 1), i - 1] = value

        return put

    inner = pl.ds(SUB, lat_cells - 2 * SUB)

    def ship(i, count):
        return pltpu.make_async_copy(
            stage.at[:, pl.ds(i - 1, count)], out.at[:, pl.ds(i, count), inner], sem.at[0]
        )

    line(0, 0, False, rim_row(0))

    def two(n, _):
        i = 1 + 2 * n
        line(i, 0, False, inner_row(i))
        line(i + 1, 1, False, inner_row(i + 1))
        ship(i, 2).start()
        return 0

    lax.fori_loop(0, (lon_cells - 2) // 2, two, 0)
    line(lon_cells - 1, 0, True, rim_row(1))
    ship(1, lon_cells - 2).wait()


def transport(mix, u_wind, v_wind, species):
    lon_cells, lat_cells, levels = u_wind.shape
    return pl.pallas_call(
        transport_kernel,
        in_specs=[VECTORS] * 3,
        out_specs=[ANYWHERE] + [VECTORS] * 2,
        out_shape=[
            pltpu.HBM((species, lon_cells, lat_cells, levels), jnp.float32),
            buffer(species, 2, lat_cells, levels),
            buffer(species, 2, lon_cells - 2, SUB, levels),
        ],
        scratch_shapes=[
            buffer(species, lat_cells, levels),
            buffer(2, species, lat_cells + SUB, levels),
            buffer(species, lon_cells - 2, lat_cells - 2 * SUB, levels),
            pltpu.SemaphoreType.DMA((1,)),
        ],
        compiler_params=pltpu.CompilerParams(vmem_limit_bytes=12 << 20),
        name="transport",
    )(in_vmem(mix), in_vmem(u_wind), in_vmem(v_wind))


def rim_kernel(
    partial, lon_rim, lat_rim, west, east, south, north, lon_tail, lon_head, lat_tail, lat_head,
    out, lon_new, lat_new, sem,
):
    species, lon_cells, lat_cells, levels = out.shape
    inner = lon_cells - 2
    wind = west[species]
    wind_out = lon_tail[species]
    place = lax.axis_index("lat")
    south_wind = jnp.where(place > 0, south[species], 0.0)
    north_wind = jnp.where(place < lax.axis_size("lat") - 1, lat_tail[species], 0.0)
    for s in range(species):
        inflow = jnp.maximum(wind, 0.0) * west[s] + jnp.minimum(wind, 0.0) * lon_head[s]
        lon_new[s, 0] = lon_rim[s, 0] + inflow
        lon_new[s, 1] = lon_rim[s, 1] - jnp.minimum(wind_out, 0.0) * east[s]
        first = jnp.maximum(south_wind, 0.0) * south[s] + jnp.minimum(south_wind, 0.0) * lat_head[s]
        final = jnp.minimum(north_wind, 0.0) * north[s]
        for side, (at, change) in enumerate(((0, first), (lat_cells - 1, -final))):
            lat_new[s, side] = lat_rim[s, side]
            for q, i in ((0, 0), (1, lon_cells - 1)):
                lon_new[s, q, pl.ds(at, 1), :] = lon_new[s, q, pl.ds(at, 1), :] + change[i : i + 1, :]
            for i in range(inner):
                spot = (s, side, i, pl.ds(at % SUB, 1))
                lat_new[spot] = lat_new[spot] + change[i + 1 : i + 2, :]
    copies = [
        pltpu.make_async_copy(lon_new.at[:, q], out.at[:, i], sem.at[q])
        for q, i in ((0, 0), (1, lon_cells - 1))
    ] + [
        pltpu.make_async_copy(
            lat_new.at[:, q], out.at[:, pl.ds(1, inner), pl.ds(start, SUB)], sem.at[2 + q]
        )
        for q, start in ((0, 0), (1, lat_cells - SUB))
    ]
    for copy in copies:
        copy.start()
    for copy in copies:
        copy.wait()


def rim_pass(partial, rims, halos, edges):
    species, lon_cells, lat_cells, levels = partial.shape
    return pl.pallas_call(
        rim_kernel,
        in_specs=[ANYWHERE] + [VECTORS] * 10,
        out_specs=ANYWHERE,
        out_shape=pltpu.HBM(partial.shape, jnp.float32),
        input_output_aliases={0: 0},
        scratch_shapes=[
            buffer(species, 2, lat_cells, levels),
            buffer(species, 2, lon_cells - 2, SUB, levels),
            pltpu.SemaphoreType.DMA((4,)),
        ],
        compiler_params=pltpu.CompilerParams(vmem_limit_bytes=12 << 20),
        name="rim",
    )(in_hbm(partial), *(in_vmem(x) for x in (*rims, *halos, *edges)))


def body(tracers, kdiff, photolysis, u_wind, v_wind, day_count, day_order):
    mix, *edges = column_pass(
        day_count.T, day_order, tracers, kdiff, photolysis, u_wind, v_wind
    )
    lon_tail, lon_head, lat_tail, lat_head = edges

    def shift(edge, axis, step):
        size = lax.axis_size(axis)
        return lax.ppermute(edge, axis, [(i, (i + step) % size) for i in range(size)])

    halos = (
        shift(lon_tail, "lon", 1),
        shift(lon_head, "lon", -1),
        shift(lat_tail, "lat", 1),
        shift(lat_head, "lat", -1),
    )
    partial, *rims = transport(mix, u_wind, v_wind, tracers.shape[0])
    return rim_pass(partial, rims, halos, edges)


def solution(mesh):
    return jax.shard_map(
        body,
        mesh=mesh,
        in_specs=(
            P(None, "lon", "lat", None),
            P("lon", "lat", None),
            P("lon", "lat", None),
            P("lon", "lat", None),
            P("lon", "lat", None),
            P(),
            P("lon", "lat", None),
        ),
        out_specs=P(None, "lon", "lat", None),
        check_vma=False,
    )
```

time: 379 us -> 51 us (0.13)
  other arithmetic: 199 us -> 0 us
  local copies, waits for them, and re-layouts: 165 us -> 0.01 us
  Pallas kernels: 0 us -> 44 us
  starting transfers between devices: 10.2 us -> 6.23 us
    add x115 -> x0, other arithmetic: 106 us -> none  [the longest x96 84.3 us: column_step(): coef_prev * current + coef_back * previous + coef_base * field]
    gather x32 -> x0, local copies, waits for them, and re-layouts: 71.6 us -> none  [the longest x8 32 us: pick_blocks(): jnp.take(blocks, block_ids, axis=1)]
    slice x192 -> x0, local copies, waits for them, and re-layouts: 64.7 us -> none  [tendency(): above = jnp.concatenate([field[..., 1:], field[..., -1:]], axis=-1)]
    pallas_call x0 -> x3, Pallas kernels: none -> 44 us  [the longest x1 37.6 us: column_pass(): pl.pallas_call(column_kernel, in_specs=[ANYWHERE] * 7, out_specs=[VECTORS...]
    mul x91 -> x0, other arithmetic: 41.8 us -> none  [the longest x88 35 us: tendency(): upward = diffusion * (above - field)]
    scatter x8 -> x0, local copies, waits for them, and re-layouts: 24.9 us -> none  [one_turn(): return running.at[:, targets].set(advanced, mode='drop')]
    sub x2 -> x0, other arithmetic: 21.9 us -> none  [the longest x1 19.6 us: body(): return current - (east - west) - (north - south)]
    another operation x96 -> x0, other arithmetic: 19.5 us -> none  [tendency(): jnp.stack([1.5 * oxygen - titration - split_o3, split_no2 + split_o3 - 1....]
  transfers between devices with their start and end apart: 4 -> 4, of which waited for: 0 -> 0; matrix products, arithmetic and copies ran while one was open for 2% -> 0% of each run, Pallas kernels for 0% -> 9%
where the time goes in v1:
time: 51 us; the launch traced here: 50.3 us
  Pallas kernels  44 us (86%)
  starting transfers between devices  6.23 us (12%)
    pallas_call x1, Pallas kernels, column_pass(): pl.pallas_call(column_kernel, in_specs=[ANYWHERE] * 7, out_specs=[VECTORS...  37.6 us
    ppermute x4, starting transfers between devices, shift(): lax.ppermute(edge, axis, [(i, (i + step) % size) for i in range(size)])  6.23 us
    pallas_call x1, Pallas kernels, transport(): pl.pallas_call(transport_kernel, in_specs=[VECTORS] * 3, out_specs=[ANYWH...  4.6 us
    pallas_call x1, Pallas kernels, rim_pass(): pl.pallas_call(rim_kernel, in_specs=[ANYWHERE] + [VECTORS] * 10, out_spec...  1.81 us
  transfers between devices with their start and end apart: 4, of which 0 were waited for; matrix products, arithmetic and copies ran while one was open for 0% of the time, Pallas kernels for 9%

profile of v1, /device:TPU:0, one launch (start us, length us, event | category | flops | bytes accessed | tf_op | source)
XLA Modules:
  0.0 50.3 jit_solution(13577684613062095470)
XLA Ops:
  0.0 0.0 copy-start
  0.0 0.0 copy-start.1
  0.0 37.6 %columns.1 = (f32[4,4224,128]{2,1,0:T(8,128)S(1)}, f32[5,64,128]{2,1,0:T(8,128)S(1)}, f32[4,64,128]{2,1,0:T(8,128)S(1)}, f32[5,64,128]{2,1,0:T(8,128)S(1)}, f32[4,64,128]{2,1,0:T(8,128)S(1)}) custom-call(s32[4,8]{1,0:T(4,128)} %bitcast.7, s32[1,1,32]{2,1,0:T(1,128)} %ranks.1, f32[4,32,128,128]{3,2,1,0:T(8,128)} %bitcast.4, f32[32,128,128]{2,1,0:T(8,128)} %bitcast.5, ...), custom_call_target="tpu_custom_call" | custom-call | tf_op jit(solution)/shard_map/columns/pallas_call | solution.py:278
  37.6 0.1 collective-permute-start
  37.7 0.1 collective-permute-start.2
  37.8 3.5 %collective-permute-start.1 = (f32[4,64,128]{2,1,0:T(8,128)S(1)}, f32[4,64,128]{2,1,0:T(8,128)S(1)}, u32[]{:S(2)}, u32[]{:S(2)}) collective-permute-start(f32[4,64,128]{2,1,0:T(8,128)S(1)} %get-tuple-element.18.lon_head), channel_id=1, source_target_pairs={{0,28},{4,0},{8,4},{12,8},{16,12},{20,16},{24,20},{28,24},{1,29},{... | collective-permute-start | bytes 393224 | tf_op jit(solution)/shard_map/ppermute | solution.py:476
  41.2 2.6 %collective-permute-start.3 = (f32[4,64,128]{2,1,0:T(8,128)S(1)}, f32[4,64,128]{2,1,0:T(8,128)S(1)}, u32[]{:S(2)}, u32[]{:S(2)}) collective-permute-start(f32[4,64,128]{2,1,0:T(8,128)S(1)} %get-tuple-element.20.lat_head), channel_id=1, source_target_pairs={{0,3},{1,0},{2,1},{3,2},{4,7},{5,4},{6,5},{7,6},{8,11},{9,8},{10,9... | collective-permute-start | bytes 393224 | tf_op jit(solution)/shard_map/ppermute | solution.py:476
  43.9 0.0 copy-done
  43.9 0.0 copy-done.1
  43.9 4.6 %transport.1 = (f32[4,64,64,128]{3,2,1,0:T(8,128)}, f32[4,2,64,128]{3,2,1,0:T(8,128)S(1)}, f32[4,2,62,8,128]{4,3,2,1,0:T(8,128)S(1)}) custom-call(f32[4,4224,128]{2,1,0:T(8,128)S(1)} %get-tuple-element.13.mix, f32[64,64,128]{2,1,0:T(8,128)S(1)} %copy-done, f32[64,64,128]{2,1,0:T(8,128)S(1)} %copy-done.1), custom_call_target="tpu_custom_call" | custom-call | tf_op jit(solution)/shard_map/transport/pallas_call | solution.py:391
  48.5 0.0 collective-permute-done.1.east
  48.5 0.0 collective-permute-done.3.north
  48.5 0.0 collective-permute-done.west
  48.5 0.0 collective-permute-done.2.south
  48.5 1.8 %rim.1 = f32[4,64,64,128]{3,2,1,0:T(8,128)} custom-call(f32[4,64,64,128]{3,2,1,0:T(8,128)} %get-tuple-element.14.partial, f32[4,2,64,128]{3,2,1,0:T(8,128)S(1)} %get-tuple-element.15.lon_rim, f32[4,2,62,8,128]{4,3,2,1,0:T(8,128)S(1)} %get-tuple-element.16.lat_rim, f32[5,64,128]{2,1,0:T(8,128)S(1)} %collective-permute-done.west, ...), custom_call_target="tpu_custom_call", output_to_operand_aliasing={{}: (0, {})} | custom-call | tf_op jit(solution)/shard_map/rim/pallas_call | solution.py:452
Async XLA Ops:
  0.0 43.9 %copy-start = (f32[64,64,128]{2,1,0:T(8,128)S(1)}, f32[64,64,128]{2,1,0:T(8,128)}, u32[]{:S(2)}) copy-start(f32[64,64,128]{2,1,0:T(8,128)} %u.3) | copy-start | bytes 6291460
  0.0 43.9 %copy-start.1 = (f32[64,64,128]{2,1,0:T(8,128)S(1)}, f32[64,64,128]{2,1,0:T(8,128)}, u32[]{:S(2)}) copy-start(f32[64,64,128]{2,1,0:T(8,128)} %v.3) | copy-start | bytes 6291460
  37.6 10.9 %collective-permute-start = (f32[5,64,128]{2,1,0:T(8,128)S(1)}, f32[5,64,128]{2,1,0:T(8,128)S(1)}, u32[]{:S(2)}, u32[]{:S(2)}) collective-permute-start(f32[5,64,128]{2,1,0:T(8,128)S(1)} %get-tuple-element.17.lon_tail), channel_id=1, source_target_pairs={{0,4},{4,8},{8,12},{12,16},{16,20},{20,24},{24,28},{28,0},{1,5},{5... | collective-permute-start | bytes 491528 | tf_op jit(solution)/shard_map/ppermute | solution.py:476
  37.7 10.8 %collective-permute-start.2 = (f32[5,64,128]{2,1,0:T(8,128)S(1)}, f32[5,64,128]{2,1,0:T(8,128)S(1)}, u32[]{:S(2)}, u32[]{:S(2)}) collective-permute-start(f32[5,64,128]{2,1,0:T(8,128)S(1)} %get-tuple-element.19.lat_tail), channel_id=1, source_target_pairs={{0,1},{1,2},{2,3},{3,0},{4,5},{5,6},{6,7},{7,4},{8,9},{9,10},{10,1... | collective-permute-start | bytes 491528 | tf_op jit(solution)/shard_map/ppermute | solution.py:476
  37.8 10.7 %collective-permute-start.1 = (f32[4,64,128]{2,1,0:T(8,128)S(1)}, f32[4,64,128]{2,1,0:T(8,128)S(1)}, u32[]{:S(2)}, u32[]{:S(2)}) collective-permute-start(f32[4,64,128]{2,1,0:T(8,128)S(1)} %get-tuple-element.18.lon_head), channel_id=1, source_target_pairs={{0,28},{4,0},{8,4},{12,8},{16,12},{20,16},{24,20},{28,24},{1,29},{... | collective-permute-start | bytes 393224 | tf_op jit(solution)/shard_map/ppermute | solution.py:476
  41.2 7.3 %collective-permute-start.3 = (f32[4,64,128]{2,1,0:T(8,128)S(1)}, f32[4,64,128]{2,1,0:T(8,128)S(1)}, u32[]{:S(2)}, u32[]{:S(2)}) collective-permute-start(f32[4,64,128]{2,1,0:T(8,128)S(1)} %get-tuple-element.20.lat_head), channel_id=1, source_target_pairs={{0,3},{1,0},{2,1},{3,2},{4,7},{5,4},{6,5},{7,6},{8,11},{9,8},{10,9... | collective-permute-start | bytes 393224 | tf_op jit(solution)/shard_map/ppermute | solution.py:476
